TPU v7x, 32 devices: a whole 2x2x4 slice. The times are simulated.
32 devices in a mesh: groups: 2 (over y), context: 4 (over z), tensor: 4 (over x, core).
Axes of the slice: x: 2, y: 2, z: 4, core: 2. Of those that a mesh axis runs over, the one named last changes fastest.
Arguments:
- inputs: bfloat16 [4096, 1024], P(('groups', 'context')), parts along dimension 0, may hold values from -6 to 6
- frame_valid: int32 [4096], P(('groups', 'context')), parts along dimension 0, may hold values from 0 to 1, as said below
- norm1_gain: float32 [1024], replicated, may hold values from 0.1 to 1.9
- w_query: bfloat16 [1024, 1024], P(None, 'tensor')
- w_key: bfloat16 [1024, 1024], P(None, 'tensor')
- w_value: bfloat16 [1024, 1024], P(None, 'tensor'), may hold values from -0.1875 to 0.1875
- w_out: bfloat16 [1024, 1024], P('tensor'), may hold values from -0.1875 to 0.1875
- norm2_gain: float32 [1024], replicated, may hold values from 0.1 to 1.9
- w_point1: bfloat16 [2, 1024, 1024], P(None, None, 'tensor'), may hold values from -0.1875 to 0.1875
- w_depth: float32 [31, 1024], P(None, 'tensor'), may hold values from -1.5 to 1.5
- bn_scale: float32 [1024], P('tensor'), may hold values from 0.1 to 1.9
- bn_shift: float32 [1024], P('tensor'), may hold values from -1 to 1
- w_point2: bfloat16 [1024, 1024], P('tensor'), may hold values from -0.1875 to 0.1875
Outputs:
- output: bfloat16 [4096, 1024], P(('groups', 'context', 'tensor')), parts along dimension 0
There are 2 independent parts, one for each index of `groups`. A program takes and returns all parts, laid end to end along the dimension named above; an argument that names none is the same for every part. Nothing has to cross between parts.
Inputs may be any that keep to these rules, and one draw needn't show every extreme that they name: `frame_valid`: the transcript frames form a prefix of the window of at least 1024 frames, followed by at least one padded frame.
All inputs are finite; a program needn't handle non-finite values.
Results may differ from a plain program's by a relative error of at most 0.0095.
Values may be sent and summed in bfloat16 or wider, within the bound.
A program may use at most 64 MiB of HBM per device.

v0:
```python
import math
import jax
import jax.numpy as jnp
from jax import lax
from jax.sharding import PartitionSpec as P

HD = 64
NEG = -1e30


def with_halo(block, sides, width):
    for axis, dim in sides:
        count = lax.axis_size(axis)
        forward = [(i, i + 1) for i in range(count - 1)]
        backward = [(target, source) for source, target in forward]
        low = lax.ppermute(
            lax.slice_in_dim(block, block.shape[dim] - width, None, axis=dim), axis, forward
        )
        high = lax.ppermute(lax.slice_in_dim(block, 0, width, axis=dim), axis, backward)
        block = jnp.concatenate([low, block, high], axis=dim)
    return block


def normalize(rows, gain):
    values = rows.astype(jnp.float32)
    center = jnp.mean(values, axis=-1, keepdims=True)
    spread = jnp.mean(jnp.square(values - center), axis=-1, keepdims=True)
    return ((values - center) * lax.rsqrt(spread + 1e-05) * gain).astype(jnp.bfloat16)


def local(
    inputs,
    frame_valid,
    norm1_gain,
    w_query,
    w_key,
    w_value,
    w_out,
    norm2_gain,
    w_point1,
    w_depth,
    bn_scale,
    bn_shift,
    w_point2,
):
    frames = inputs.shape[0]
    local_cols = w_query.shape[1]
    head_dim = HD
    heads_here = local_cols // head_dim
    scale = 1.0 / math.sqrt(head_dim)
    normed = normalize(inputs, norm1_gain)
    query = jnp.dot(normed, w_query, preferred_element_type=jnp.float32).astype(jnp.bfloat16)
    query = query.reshape(frames, heads_here, head_dim)
    keys = jnp.dot(normed, w_key, preferred_element_type=jnp.float32).astype(jnp.bfloat16)
    vals = jnp.dot(normed, w_value, preferred_element_type=jnp.float32).astype(jnp.bfloat16)

    def update(carry, key_blk, val_blk, valid_blk):
        run_max, run_sum, accum = carry
        rows = key_blk.shape[0]
        key_heads = key_blk.reshape(rows, heads_here, head_dim)
        val_heads = val_blk.reshape(rows, heads_here, head_dim)
        scores = (
            jnp.einsum("qhd,khd->hqk", query, key_heads, preferred_element_type=jnp.float32) * scale
        )
        live = (valid_blk > 0)[None, None, :]
        scores = jnp.where(live, scores, NEG)
        new_max = jnp.maximum(run_max, jnp.max(scores, axis=-1))
        weights = jnp.where(live, jnp.exp(scores - new_max[:, :, None]), 0.0)
        factor = jnp.exp(run_max - new_max)
        run_sum = run_sum * factor + jnp.sum(weights, axis=-1)
        mixed = jnp.einsum(
            "hqk,khd->qhd",
            weights.astype(jnp.bfloat16),
            val_heads,
            preferred_element_type=jnp.float32,
        )
        accum = accum * jnp.repeat(factor.T, head_dim, axis=1) + mixed.reshape(frames, local_cols)
        return (new_max, run_sum, accum)

    def visit(carry, key_blk, val_blk, valid_blk):
        return update(carry, key_blk, val_blk, valid_blk)

    start_state = (
        jnp.full((heads_here, frames), NEG, jnp.float32),
        jnp.zeros((heads_here, frames), jnp.float32),
        jnp.zeros((frames, local_cols), jnp.float32),
    )
    carry = start_state
    key_part = lax.all_gather(keys, "context", axis=0, tiled=True)
    val_part = lax.all_gather(vals, "context", axis=0, tiled=True)
    valid_part = lax.all_gather(frame_valid, "context", axis=0, tiled=True)
    rows = key_part.shape[0]
    shards = max(rows // frames, 1)
    group = math.gcd(shards, max(1536 // frames, 1))
    blocks = shards // group
    block_rows = rows // blocks

    def advance(state, items):
        return (visit(state, items[0], items[1], items[2]), None)

    stacked = (
        key_part.reshape(blocks, block_rows, local_cols),
        val_part.reshape(blocks, block_rows, local_cols),
        valid_part.reshape(blocks, block_rows),
    )
    carry, unused = lax.scan(advance, carry, stacked)
    run_max, run_sum, accum = carry
    attended = (accum / jnp.repeat(run_sum.T, head_dim, axis=1)).astype(jnp.bfloat16)
    share = frames // lax.axis_size("tensor")
    first_row = lax.axis_index("tensor") * share
    total = lax.psum(jnp.dot(attended, w_out, preferred_element_type=jnp.float32), "tensor")
    residual = (inputs.astype(jnp.float32) + total).astype(jnp.bfloat16)
    normed_two = normalize(residual, norm2_gain)
    residual_rows = lax.dynamic_slice_in_dim(residual, first_row, share, 0)
    value_half = jnp.dot(normed_two, w_point1[0], preferred_element_type=jnp.float32)
    gate_half = jnp.dot(normed_two, w_point1[1], preferred_element_type=jnp.float32)
    gated = jnp.where(
        (frame_valid > 0)[:, None], value_half * jax.nn.sigmoid(gate_half), 0.0
    ).astype(jnp.bfloat16)
    taps = w_depth.shape[0]
    half = (taps - 1) // 2
    padded = with_halo(gated, (("context", 0),), half)
    depth = jnp.zeros((frames, gated.shape[1]), jnp.float32)
    for tap in range(taps):
        depth = depth + padded[tap : tap + frames].astype(jnp.float32) * w_depth[tap]
    activated = jax.nn.silu(depth * bn_scale + bn_shift).astype(jnp.bfloat16)
    conv_rows = lax.psum_scatter(
        jnp.dot(activated, w_point2, preferred_element_type=jnp.float32).astype(jnp.bfloat16),
        "tensor",
        scatter_dimension=0,
        tiled=True,
    ).astype(jnp.float32)
    return (residual_rows.astype(jnp.float32) + conv_rows).astype(jnp.bfloat16)


def solution(mesh):
    placed = (
        P(("groups", "context"), None),
        P(("groups", "context")),
        P(),
        P(None, "tensor"),
        P(None, "tensor"),
        P(None, "tensor"),
        P("tensor", None),
        P(),
        P(None, None, "tensor"),
        P(None, "tensor"),
        P("tensor"),
        P("tensor"),
        P("tensor", None),
    )
    return jax.shard_map(
        local,
        mesh=mesh,
        in_specs=placed,
        out_specs=P(("groups", "context", "tensor"), None),
        check_vma=False,
    )
```

profile of v0, /device:TPU:0, one launch (start us, length us, event | category | flops | bytes accessed | tf_op | source)
XLA Modules:
  0.0 218.2 jit_solution(7202695658550756041)
XLA Ops:
  6.5 0.0 all-gather.4.cloned.1.call-start
  6.6 1.6 convert_reduce_fusion
  8.2 1.6 fusion.17
  9.9 1.2 convolution_convert_fusion.3
  11.1 0.0 all-gather.4.cloned.1.call-update
  11.1 0.0 all-gather.6.cloned.1.call-start
  11.2 1.2 convolution_convert_fusion.1
  12.4 0.0 all-gather.6.cloned.1.call-update
  12.4 0.0 all-reduce.2.cloned.1.call-start
  12.5 13.7 %all-gather = s32[4,1,512]{2,1,0:T(1,128)S(1)} all-gather(s32[1,1,512]{2,1,0:T(1,128)S(1)} %bitcast.111), channel_id=1, replica_groups=mesh['groups'=2,'context'=4,'tensor'=4] {'context'}, dimensions={0}, use_global_device_ids=true | all-gather | bytes 10240 | tf_op jit(solution)/shard_map/all_gather | solution.py:91
  26.2 1.7 convolution_convert_fusion.2
  27.9 14.0 %all-gather.4.cloned.1.call-done = bf16[2048,256]{1,0:T(8,128)(2,1)} async-done(((bf16[512,256]{1,0:T(8,128)(2,1)}), bf16[2048,256]{1,0:T(8,128)(2,1)}) %all-gather.4.cloned.1.call-update) | async-done | bytes 1048592 | tf_op jit(solution)/shard_map/all_gather | solution.py:89
  41.9 29.0 %all-gather.6.cloned.1.call-done = bf16[2048,256]{1,0:T(8,128)(2,1)} async-done(((bf16[512,256]{1,0:T(8,128)(2,1)}), bf16[2048,256]{1,0:T(8,128)(2,1)}) %all-gather.6.cloned.1.call-update) | async-done | bytes 1048592 | tf_op jit(solution)/shard_map/all_gather | solution.py:90
  70.9 44.4 %while.15 = (s32[]{:T(128)}, f32[4,512]{1,0:T(4,128)S(1)}, f32[4,512]{1,0:T(4,128)S(1)}, f32[512,256]{0,1:T(8,128)S(1)}, s32[4,512]{1,0:T(4,128)S(1)}, /*index=5...) while((s32[]{:T(128)}, f32[4,512]{1,0:T(4,128)S(1)}, ...), condition=%wide.region_5.6_spmd.clone, body=%wide.region_2.5_spmd.clone.sunk | while | flops 282472960 | bytes 17698944 | solution.py:106
  71.0 1.1 constant_dynamic-slice_fusion.3
  72.0 0.1 copy.28
  72.2 2.9 %bitcast_reduce_fusion.2 = (f32[4,512]{1,0:T(4,128)S(1)}, f32[4,512,512]{2,1,0:T(8,128)}) fusion(pred[512]{0:T(512)(128)(4,1)S(1)} %compare_reduce_fusion.2, bf16[512,4,64]{0,2,1:T(8,128)(2,1)S(1)} %bitcast.104, bf16[512,4,64]{0,2,1:T(8,128)(2,1)S(1)} %get-tuple-element.237), kind=kOutput, calls=%fused_computation.1.clone.1 | convolution fusion | flops 137361408 | bytes 4727296 | tf_op jit(solution)/shard_map/while/body/eval_jaxpr/qhd,khd->hqk/dot_general | solution.py:63
  75.1 3.3 %fusion.96 = f32[4,512]{1,0:T(4,128)S(1)} fusion(f32[4,512,512]{2,1,0:T(8,128)} %get-tuple-element.208, f32[4,512]{1,0:T(4,128)S(1)} %get-tuple-element.232, pred[512]{0:T(512)(128)(4,1)S(1)} %compare_reduce_fusion.2), kind=kLoop, calls=%fused_computation.6.clone.1 | loop fusion | flops 5240832 | bytes 4211200 | tf_op jit(solution)/shard_map/while/body/eval_jaxpr/reduce_sum | solution.py:70
  78.4 0.1 copy.29
  78.6 3.3 %fusion.98 = f32[4,64,512]{2,1,0:T(8,128)S(1)} fusion(bf16[512,4,64]{0,2,1:T(8,128)(2,1)S(1)} %bitcast.106, f32[4,512,512]{2,1,0:T(8,128)} %get-tuple-element.208, f32[4,512]{1,0:T(4,128)S(1)} %get-tuple-element.232, pred[512]{0:T(512)(128)(4,1)S(1)} %compare_reduce_fusion.2), kind=kOutput, calls=%fused_computation.7.clone.1 | convolution fusion | flops 139460608 | bytes 4989440 | tf_op jit(solution)/shard_map/while/body/eval_jaxpr/hqk,khd->qhd/dot_general | solution.py:71
  81.8 0.2 bitcast_add_fusion.2
  82.1 1.1 constant_dynamic-slice_fusion.3
  83.1 0.1 copy.28
  83.3 2.9 %bitcast_reduce_fusion.2 = (f32[4,512]{1,0:T(4,128)S(1)}, f32[4,512,512]{2,1,0:T(8,128)}) fusion(pred[512]{0:T(512)(128)(4,1)S(1)} %compare_reduce_fusion.2, bf16[512,4,64]{0,2,1:T(8,128)(2,1)S(1)} %bitcast.104, bf16[512,4,64]{0,2,1:T(8,128)(2,1)S(1)} %get-tuple-element.237), kind=kOutput, calls=%fused_computation.1.clone.1 | convolution fusion | flops 137361408 | bytes 4727296 | tf_op jit(solution)/shard_map/while/body/eval_jaxpr/qhd,khd->hqk/dot_general | solution.py:63
  86.2 3.3 %fusion.96 = f32[4,512]{1,0:T(4,128)S(1)} fusion(f32[4,512,512]{2,1,0:T(8,128)} %get-tuple-element.208, f32[4,512]{1,0:T(4,128)S(1)} %get-tuple-element.232, pred[512]{0:T(512)(128)(4,1)S(1)} %compare_reduce_fusion.2), kind=kLoop, calls=%fused_computation.6.clone.1 | loop fusion | flops 5240832 | bytes 4211200 | tf_op jit(solution)/shard_map/while/body/eval_jaxpr/reduce_sum | solution.py:70
  89.5 0.1 copy.29
  89.7 3.3 %fusion.98 = f32[4,64,512]{2,1,0:T(8,128)S(1)} fusion(bf16[512,4,64]{0,2,1:T(8,128)(2,1)S(1)} %bitcast.106, f32[4,512,512]{2,1,0:T(8,128)} %get-tuple-element.208, f32[4,512]{1,0:T(4,128)S(1)} %get-tuple-element.232, pred[512]{0:T(512)(128)(4,1)S(1)} %compare_reduce_fusion.2), kind=kOutput, calls=%fused_computation.7.clone.1 | convolution fusion | flops 139460608 | bytes 4989440 | tf_op jit(solution)/shard_map/while/body/eval_jaxpr/hqk,khd->qhd/dot_general | solution.py:71
  92.9 0.2 bitcast_add_fusion.2
  93.2 1.1 constant_dynamic-slice_fusion.3
  94.2 0.1 copy.28
  94.4 2.9 %bitcast_reduce_fusion.2 = (f32[4,512]{1,0:T(4,128)S(1)}, f32[4,512,512]{2,1,0:T(8,128)}) fusion(pred[512]{0:T(512)(128)(4,1)S(1)} %compare_reduce_fusion.2, bf16[512,4,64]{0,2,1:T(8,128)(2,1)S(1)} %bitcast.104, bf16[512,4,64]{0,2,1:T(8,128)(2,1)S(1)} %get-tuple-element.237), kind=kOutput, calls=%fused_computation.1.clone.1 | convolution fusion | flops 137361408 | bytes 4727296 | tf_op jit(solution)/shard_map/while/body/eval_jaxpr/qhd,khd->hqk/dot_general | solution.py:63
  97.3 3.3 %fusion.96 = f32[4,512]{1,0:T(4,128)S(1)} fusion(f32[4,512,512]{2,1,0:T(8,128)} %get-tuple-element.208, f32[4,512]{1,0:T(4,128)S(1)} %get-tuple-element.232, pred[512]{0:T(512)(128)(4,1)S(1)} %compare_reduce_fusion.2), kind=kLoop, calls=%fused_computation.6.clone.1 | loop fusion | flops 5240832 | bytes 4211200 | tf_op jit(solution)/shard_map/while/body/eval_jaxpr/reduce_sum | solution.py:70
  100.6 0.1 copy.29
  100.8 3.3 %fusion.98 = f32[4,64,512]{2,1,0:T(8,128)S(1)} fusion(bf16[512,4,64]{0,2,1:T(8,128)(2,1)S(1)} %bitcast.106, f32[4,512,512]{2,1,0:T(8,128)} %get-tuple-element.208, f32[4,512]{1,0:T(4,128)S(1)} %get-tuple-element.232, pred[512]{0:T(512)(128)(4,1)S(1)} %compare_reduce_fusion.2), kind=kOutput, calls=%fused_computation.7.clone.1 | convolution fusion | flops 139460608 | bytes 4989440 | tf_op jit(solution)/shard_map/while/body/eval_jaxpr/hqk,khd->qhd/dot_general | solution.py:71
  104.1 0.2 bitcast_add_fusion.2
  104.3 1.1 constant_dynamic-slice_fusion.3
  105.3 0.1 copy.28
  105.5 2.9 %bitcast_reduce_fusion.2 = (f32[4,512]{1,0:T(4,128)S(1)}, f32[4,512,512]{2,1,0:T(8,128)}) fusion(pred[512]{0:T(512)(128)(4,1)S(1)} %compare_reduce_fusion.2, bf16[512,4,64]{0,2,1:T(8,128)(2,1)S(1)} %bitcast.104, bf16[512,4,64]{0,2,1:T(8,128)(2,1)S(1)} %get-tuple-element.237), kind=kOutput, calls=%fused_computation.1.clone.1 | convolution fusion | flops 137361408 | bytes 4727296 | tf_op jit(solution)/shard_map/while/body/eval_jaxpr/qhd,khd->hqk/dot_general | solution.py:63
  108.4 3.3 %fusion.96 = f32[4,512]{1,0:T(4,128)S(1)} fusion(f32[4,512,512]{2,1,0:T(8,128)} %get-tuple-element.208, f32[4,512]{1,0:T(4,128)S(1)} %get-tuple-element.232, pred[512]{0:T(512)(128)(4,1)S(1)} %compare_reduce_fusion.2), kind=kLoop, calls=%fused_computation.6.clone.1 | loop fusion | flops 5240832 | bytes 4211200 | tf_op jit(solution)/shard_map/while/body/eval_jaxpr/reduce_sum | solution.py:70
  111.7 0.1 copy.29
  111.9 3.3 %fusion.98 = f32[4,64,512]{2,1,0:T(8,128)S(1)} fusion(bf16[512,4,64]{0,2,1:T(8,128)(2,1)S(1)} %bitcast.106, f32[4,512,512]{2,1,0:T(8,128)} %get-tuple-element.208, f32[4,512]{1,0:T(4,128)S(1)} %get-tuple-element.232, pred[512]{0:T(512)(128)(4,1)S(1)} %compare_reduce_fusion.2), kind=kOutput, calls=%fused_computation.7.clone.1 | convolution fusion | flops 139460608 | bytes 4989440 | tf_op jit(solution)/shard_map/while/body/eval_jaxpr/hqk,khd->qhd/dot_general | solution.py:71
  115.2 0.2 bitcast_add_fusion.2
  115.4 0.1 fusion.31
  115.4 0.0 copy-start.2
  115.4 1.8 fusion.73
  117.2 0.0 all-reduce.2.cloned.1.call-update
  117.2 0.0 reduce-scatter.2.cloned.1.call-start
  117.3 0.0 copy-start.9
  117.4 50.9 %all-reduce.2.cloned.1.call-done = f32[512,1024]{1,0:T(8,128)} async-done(((f32[512,1024]{1,0:T(8,128)}), f32[512,1024]{1,0:T(8,128)}) %all-reduce.2.cloned.1.call-update) | async-done | bytes 2097168 | tf_op jit(solution)/shard_map/psum | solution.py:111
  168.3 2.0 convert_reduce_fusion.1
  170.3 0.4 fusion.20
  170.7 0.5 fusion.27
  171.3 0.0 copy-start.7
  171.3 0.0 copy-start.10
  171.3 0.0 copy-start.11
  171.3 0.5 fusion.28
  171.9 1.3 collective-permute-start.1
  173.2 4.5 %collective-permute-start = (bf16[15,256]{1,0:T(8,128)(2,1)S(1)}, bf16[15,256]{1,0:T(8,128)(2,1)S(1)}, u32[]{:S(2)}, u32[]{:S(2)}) collective-permute-start(bf16[15,256]{1,0:T(8,128)(2,1)S(1)} %get-tuple-element.117), channel_id=1, source_target_pairs={{0,4},{4,8},{8,12},{1,5},{5,9},{9,13},{2,6},{6,10},{10,14},{3,7},{... | collective-permute-start | bytes 23048 | tf_op jit(solution)/shard_map/ppermute | solution.py:16
  177.7 0.0 collective-permute-done.1
  177.7 1.3 collective-permute-done
  179.1 4.9 %convolution_convert_fusion = bf16[512,1024]{1,0:T(8,128)(2,1)} fusion(bf16[256,1024]{1,0:T(8,128)(2,1)S(1)} %copy-done.7, bf16[512,256]{1,0:T(8,128)(2,1)S(1)} %fusion.28, bf16[15,256]{1,0:T(8,128)(2,1)S(1)} %collective-permute-done.1, bf16[15,256]{1,0:T(8,128)(2,1)S(1)} %collective-permute-done, f32[256]{0:T(256)S(1)} %copy-done.10, ...), kind=kOutput, calls=%fused_computation.67 | convolution fusion | flops 293732352 | bytes 1884160 | tf_op jit(solution)/shard_map/dot_general | solution.py:128
  183.9 0.0 reduce-scatter.2.cloned.1.call-update
  184.0 26.0 %reduce-scatter.2.cloned.1.call-done = bf16[128,1024]{1,0:T(8,128)(2,1)} async-done(((bf16[512,1024]{1,0:T(8,128)(2,1)}), bf16[128,1024]{1,0:T(8,128)(2,1)}) %reduce-scatter.2.cloned.1.call-update) | async-done | bytes 262160 | tf_op jit(solution)/shard_map/reduce_scatter | solution.py:127
  209.9 1.7 add_convert_fusion
  (47 shorter events, 0.4 us)
Async XLA Ops:
  6.5 108.9 %copy-start = (bf16[256,1024]{1,0:T(8,128)(2,1)S(1)}, bf16[256,1024]{1,0:T(8,128)(2,1)}, u32[]{:S(2)}) copy-start(bf16[256,1024]{1,0:T(8,128)(2,1)} %param.21) | copy-start | bytes 1572868
  6.5 3.3 %copy-start.1 = (bf16[512,1024]{1,0:T(8,128)(2,1)S(1)}, bf16[512,1024]{1,0:T(8,128)(2,1)}, u32[]{:S(2)}) copy-start(bf16[512,1024]{1,0:T(8,128)(2,1)} %param.15) | copy-start | bytes 3145732
  6.5 3.3 %copy-start.5 = (bf16[1024,256]{1,0:T(8,128)(2,1)S(1)}, bf16[1024,256]{1,0:T(8,128)(2,1)}, u32[]{:S(2)}) copy-start(bf16[1024,256]{1,0:T(8,128)(2,1)} %param.19) | copy-start | bytes 1572868
  6.5 3.3 %copy-start.8 = (f32[1024]{0:T(1024)S(1)}, f32[1024]{0:T(1024)}, u32[]{:S(2)}) copy-start(f32[1024]{0:T(1024)} %param.17) | copy-start | bytes 12292
  6.5 35.4 %all-gather.4.cloned.1.call-start = ((), (), s32[]{:S(2)}) async-start(), calls=%async_computation.1 | async-start | bytes 1310720 | tf_op jit(solution)/shard_map/all_gather | solution.py:89
  9.8 1.4 copy-start.6
  11.1 1.4 copy-start.3
  11.1 59.8 %all-gather.6.cloned.1.call-start = ((), (), s32[]{:S(2)}) async-start(), calls=%async_computation.2 | async-start | bytes 1310720 | tf_op jit(solution)/shard_map/all_gather | solution.py:90
  12.4 155.9 %all-reduce.2.cloned.1.call-start = ((), (), s32[]{:S(2)}) async-start(), calls=%async_computation.3 | async-start | bytes 4194304 | tf_op jit(solution)/shard_map/psum | solution.py:111
  115.4 1.9 copy-start.2
  117.2 92.7 %reduce-scatter.2.cloned.1.call-start = ((), (), s32[]{:S(2)}) async-start(), calls=%async_computation.4 | async-start | bytes 1310720 | tf_op jit(solution)/shard_map/reduce_scatter | solution.py:127
  117.3 53.4 %copy-start.9 = (f32[1024]{0:T(1024)S(1)}, f32[1024]{0:T(1024)}, u32[]{:S(2)}) copy-start(f32[1024]{0:T(1024)} %param.22) | copy-start | bytes 12292
  168.3 2.4 %copy-start.4 = (bf16[2,1024,256]{2,1,0:T(8,128)(2,1)S(1)}, bf16[2,1024,256]{2,1,0:T(8,128)(2,1)}, u32[]{:S(2)}) copy-start(bf16[2,1024,256]{2,1,0:T(8,128)(2,1)} %param.23) | copy-start | bytes 3145732
  171.3 7.8 %copy-start.7 = (bf16[256,1024]{1,0:T(8,128)(2,1)S(1)}, bf16[256,1024]{1,0:T(8,128)(2,1)}, u32[]{:S(2)}) copy-start(bf16[256,1024]{1,0:T(8,128)(2,1)} %param.27) | copy-start | bytes 1572868
  171.3 7.8 %copy-start.10 = (f32[256]{0:T(256)S(1)}, f32[256]{0:T(256)}, u32[]{:S(2)}) copy-start(f32[256]{0:T(256)} %param.26) | copy-start | bytes 3076
  171.3 7.8 %copy-start.11 = (f32[256]{0:T(256)S(1)}, f32[256]{0:T(256)}, u32[]{:S(2)}) copy-start(f32[256]{0:T(256)} %param.25) | copy-start | bytes 3076
  171.9 5.9 %collective-permute-start.1 = (bf16[15,256]{1,0:T(8,128)(2,1)S(1)}, bf16[15,256]{1,0:T(8,128)(2,1)S(1)}, u32[]{:S(2)}, u32[]{:S(2)}) collective-permute-start(bf16[15,256]{1,0:T(8,128)(2,1)S(1)} %get-tuple-element.118), channel_id=1, source_target_pairs={{4,0},{8,4},{12,8},{5,1},{9,5},{13,9},{6,2},{10,6},{14,10},{7,3},{... | collective-permute-start | bytes 23048 | tf_op jit(solution)/shard_map/ppermute | solution.py:19
  173.2 5.9 %collective-permute-start = (bf16[15,256]{1,0:T(8,128)(2,1)S(1)}, bf16[15,256]{1,0:T(8,128)(2,1)S(1)}, u32[]{:S(2)}, u32[]{:S(2)}) collective-permute-start(bf16[15,256]{1,0:T(8,128)(2,1)S(1)} %get-tuple-element.117), channel_id=1, source_target_pairs={{0,4},{4,8},{8,12},{1,5},{5,9},{9,13},{2,6},{6,10},{10,14},{3,7},{... | collective-permute-start | bytes 23048 | tf_op jit(solution)/shard_map/ppermute | solution.py:16
Sparse Core Ops, SparseCore 0:
  11.2 30.6 all-gather.3
  43.5 27.3 all-gather.5
  117.4 50.8 all-reduce.1
  184.1 25.8 reduce-scatter.1
where the time goes:
time: 219 us; the launch traced here: 218 us
  waiting for transfers between devices  121 us (55%)
  matrix products  36.7 us (17%)
  other arithmetic  21.4 us (10%)
  blocking collectives  13.7 us (6%)
  between operations  13.4 us (6%)
  starting transfers between devices  6 us (3%)
  local copies, waits for them, and re-layouts  5.5 us (3%)
    psum x1, waiting for transfers between devices, local(): lax.psum(jnp.dot(attended, w_out, preferred_element_type=jnp.float32), 't...  50.9 us
    all_gather x1, waiting for transfers between devices, local(): val_part = lax.all_gather(vals, 'context', axis=0, tiled=True)  29 us
    reduce_scatter x1, waiting for transfers between devices, local(): lax.psum_scatter(jnp.dot(activated, w_point2, preferred_element_type=jnp....  26 us
    all_gather x1, waiting for transfers between devices, local(): key_part = lax.all_gather(keys, 'context', axis=0, tiled=True)  14 us
    all_gather x1, blocking collectives, local(): valid_part = lax.all_gather(frame_valid, 'context', axis=0, tiled=True)  13.7 us
    dot_general x4, matrix products, update(): jnp.einsum('hqk,khd->qhd', weights.astype(jnp.bfloat16), val_heads, prefe...  13.1 us
    reduce_sum x4, other arithmetic, update(): run_sum = run_sum * factor + jnp.sum(weights, axis=-1)  13.1 us
    dot_general x4, matrix products, update(): jnp.einsum('qhd,khd->hqk', query, key_heads, preferred_element_type=jnp.f...  11.6 us
  transfers between devices with their start and end apart: 6, of which 5 were waited for; matrix products, arithmetic and copies ran while one was open for 1% of the time, Pallas kernels for 0%

commit v1 on v0

--- a/solution.py
+++ b/solution.py
@@ -108,7 +108,9 @@
     attended = (accum / jnp.repeat(run_sum.T, head_dim, axis=1)).astype(jnp.bfloat16)
     share = frames // lax.axis_size("tensor")
     first_row = lax.axis_index("tensor") * share
-    total = lax.psum(jnp.dot(attended, w_out, preferred_element_type=jnp.float32), "tensor")
+    part = jnp.dot(attended, w_out, preferred_element_type=jnp.float32)
+    shards_2 = lax.all_gather(part, "tensor", axis=0, tiled=False)
+    total = shards_2.sum(axis=0)
     residual = (inputs.astype(jnp.float32) + total).astype(jnp.bfloat16)
     normed_two = normalize(residual, norm2_gain)
     residual_rows = lax.dynamic_slice_in_dim(residual, first_row, share, 0)

time: 219 us -> 224 us (1.023)
  waiting for transfers between devices: 121 us -> 129 us
  other arithmetic: 21.4 us -> 18.9 us
    all_gather x0 -> x1, waiting for transfers between devices: none -> 57.8 us  [local(): shards_2 = lax.all_gather(part, 'tensor', axis=0, tiled=False)]
    psum x1 -> x0, waiting for transfers between devices: 50.9 us -> none  [local(): lax.psum(jnp.dot(attended, w_out, preferred_element_type=jnp.float32), 't...]
    reduce_sum x4, other arithmetic: 13.1 us -> 4.64 us  [update(): run_sum = run_sum * factor + jnp.sum(weights, axis=-1)]
    reduce_sum x0 -> x1, other arithmetic: none -> 5.93 us  [local(): total = shards_2.sum(axis=0)]
    ppermute x1, waiting for transfers between devices: 0.01 us -> 4.2 us  [with_halo(): lax.ppermute(lax.slice_in_dim(block, 0, width, axis=dim), axis, backward)]
where the time goes in v1:
time: 224 us; the launch traced here: 223 us
  waiting for transfers between devices  129 us (58%)
  matrix products  37.4 us (17%)
  other arithmetic  18.9 us (8%)
  blocking collectives  13.7 us (6%)
  between operations  13.4 us (6%)
  local copies, waits for them, and re-layouts  5.52 us (2%)
  starting transfers between devices  4.84 us (2%)
    all_gather x1, waiting for transfers between devices, local(): shards_2 = lax.all_gather(part, 'tensor', axis=0, tiled=False)  57.8 us
    all_gather x1, waiting for transfers between devices, local(): val_part = lax.all_gather(vals, 'context', axis=0, tiled=True)  29 us
    reduce_scatter x1, waiting for transfers between devices, local(): lax.psum_scatter(jnp.dot(activated, w_point2, preferred_element_type=jnp....  24.1 us
    all_gather x1, waiting for transfers between devices, local(): key_part = lax.all_gather(keys, 'context', axis=0, tiled=True)  14 us
    dot_general x4, matrix products, update(): jnp.einsum('hqk,khd->qhd', weights.astype(jnp.bfloat16), val_heads, prefe...  13.8 us
    all_gather x1, blocking collectives, local(): valid_part = lax.all_gather(frame_valid, 'context', axis=0, tiled=True)  13.7 us
    dot_general x4, matrix products, update(): jnp.einsum('qhd,khd->hqk', query, key_heads, preferred_element_type=jnp.f...  11.6 us
    reduce_sum x1, other arithmetic, local(): total = shards_2.sum(axis=0)  5.93 us
  transfers between devices with their start and end apart: 6, of which 5 were waited for; matrix products, arithmetic and copies ran while one was open for 1% of the time, Pallas kernels for 0%

profile of v1, /device:TPU:0, one launch (start us, length us, event | category | flops | bytes accessed | tf_op | source)
XLA Modules:
  0.0 223.3 jit_solution(12946484165938280765)
XLA Ops:
  6.5 0.0 all-gather.6.cloned.1.call-start
  6.6 1.6 convert_reduce_fusion
  8.2 1.6 fusion.17
  9.9 1.2 convolution_convert_fusion.3
  11.1 0.0 all-gather.6.cloned.1.call-update
  11.1 0.0 all-gather.8.cloned.1.call-start
  11.2 1.2 convolution_convert_fusion.1
  12.4 0.0 all-gather.8.cloned.1.call-update
  12.4 0.0 all-gather.10.cloned.1.call-start
  12.5 13.7 %all-gather.1 = s32[4,1,512]{2,1,0:T(1,128)S(1)} all-gather(s32[1,1,512]{2,1,0:T(1,128)S(1)} %bitcast.113), channel_id=1, replica_groups=mesh['groups'=2,'context'=4,'tensor'=4] {'context'}, dimensions={0}, use_global_device_ids=true | all-gather | bytes 10240 | tf_op jit(solution)/shard_map/all_gather | solution.py:91
  26.2 1.7 convolution_convert_fusion.2
  27.9 14.0 %all-gather.6.cloned.1.call-done = bf16[2048,256]{1,0:T(8,128)(2,1)} async-done(((bf16[512,256]{1,0:T(8,128)(2,1)}), bf16[2048,256]{1,0:T(8,128)(2,1)}) %all-gather.6.cloned.1.call-update) | async-done | bytes 1048592 | tf_op jit(solution)/shard_map/all_gather | solution.py:89
  41.9 29.0 %all-gather.8.cloned.1.call-done = bf16[2048,256]{1,0:T(8,128)(2,1)} async-done(((bf16[512,256]{1,0:T(8,128)(2,1)}), bf16[2048,256]{1,0:T(8,128)(2,1)}) %all-gather.8.cloned.1.call-update) | async-done | bytes 1048592 | tf_op jit(solution)/shard_map/all_gather | solution.py:90
  70.9 36.7 %while.15 = (s32[]{:T(128)}, f32[4,512]{1,0:T(4,128)S(1)}, f32[4,512]{1,0:T(4,128)S(1)}, f32[512,256]{0,1:T(8,128)S(1)}, s32[4,512]{1,0:T(4,128)S(1)}, /*index=5...) while((s32[]{:T(128)}, f32[4,512]{1,0:T(4,128)S(1)}, ...), condition=%wide.region_5.6_spmd.clone, body=%wide.region_2.5_spmd.clone.sunk | while | flops 282472960 | bytes 34476180 | solution.py:106
  70.9 1.1 constant_dynamic-slice_fusion.3
  72.0 0.1 copy.28
  72.2 2.9 %bitcast_reduce_fusion.2 = (f32[4,512]{1,0:T(4,128)S(1)}, f32[4,512,512]{2,1,0:T(8,128)}) fusion(pred[512]{0:T(512)(128)(4,1)S(1)} %compare_reduce_fusion.2, bf16[512,4,64]{0,2,1:T(8,128)(2,1)S(1)} %bitcast.105, bf16[512,4,64]{0,2,1:T(8,128)(2,1)S(1)} %get-tuple-element.237), kind=kOutput, calls=%fused_computation.1.clone.1 | convolution fusion | flops 137361408 | bytes 4727296 | tf_op jit(solution)/shard_map/while/body/eval_jaxpr/qhd,khd->hqk/dot_general | solution.py:63
  75.1 0.1 copy.29
  75.3 3.4 %fusion.98 = f32[4,64,512]{2,1,0:T(8,128)S(1)} fusion(bf16[512,4,64]{0,2,1:T(8,128)(2,1)S(1)} %bitcast.108, f32[4,512,512]{2,1,0:T(8,128)} %get-tuple-element.208, f32[4,512]{1,0:T(4,128)S(1)} %get-tuple-element.232, pred[512]{0:T(512)(128)(4,1)S(1)} %compare_reduce_fusion.2), kind=kOutput, calls=%fused_computation.7.clone.1 | convolution fusion | flops 139460608 | bytes 4989440 | tf_op jit(solution)/shard_map/while/body/eval_jaxpr/hqk,khd->qhd/dot_general | solution.py:71
  78.7 0.2 bitcast_add_fusion.2
  78.9 1.2 fusion.96
  80.1 1.1 constant_dynamic-slice_fusion.3
  81.2 0.1 copy.28
  81.4 2.9 %bitcast_reduce_fusion.2 = (f32[4,512]{1,0:T(4,128)S(1)}, f32[4,512,512]{2,1,0:T(8,128)}) fusion(pred[512]{0:T(512)(128)(4,1)S(1)} %compare_reduce_fusion.2, bf16[512,4,64]{0,2,1:T(8,128)(2,1)S(1)} %bitcast.105, bf16[512,4,64]{0,2,1:T(8,128)(2,1)S(1)} %get-tuple-element.237), kind=kOutput, calls=%fused_computation.1.clone.1 | convolution fusion | flops 137361408 | bytes 4727296 | tf_op jit(solution)/shard_map/while/body/eval_jaxpr/qhd,khd->hqk/dot_general | solution.py:63
  84.3 0.1 copy.29
  84.4 3.4 %fusion.98 = f32[4,64,512]{2,1,0:T(8,128)S(1)} fusion(bf16[512,4,64]{0,2,1:T(8,128)(2,1)S(1)} %bitcast.108, f32[4,512,512]{2,1,0:T(8,128)} %get-tuple-element.208, f32[4,512]{1,0:T(4,128)S(1)} %get-tuple-element.232, pred[512]{0:T(512)(128)(4,1)S(1)} %compare_reduce_fusion.2), kind=kOutput, calls=%fused_computation.7.clone.1 | convolution fusion | flops 139460608 | bytes 4989440 | tf_op jit(solution)/shard_map/while/body/eval_jaxpr/hqk,khd->qhd/dot_general | solution.py:71
  87.9 0.2 bitcast_add_fusion.2
  88.1 1.2 fusion.96
  89.3 1.1 constant_dynamic-slice_fusion.3
  90.3 0.1 copy.28
  90.5 2.9 %bitcast_reduce_fusion.2 = (f32[4,512]{1,0:T(4,128)S(1)}, f32[4,512,512]{2,1,0:T(8,128)}) fusion(pred[512]{0:T(512)(128)(4,1)S(1)} %compare_reduce_fusion.2, bf16[512,4,64]{0,2,1:T(8,128)(2,1)S(1)} %bitcast.105, bf16[512,4,64]{0,2,1:T(8,128)(2,1)S(1)} %get-tuple-element.237), kind=kOutput, calls=%fused_computation.1.clone.1 | convolution fusion | flops 137361408 | bytes 4727296 | tf_op jit(solution)/shard_map/while/body/eval_jaxpr/qhd,khd->hqk/dot_general | solution.py:63
  93.4 0.1 copy.29
  93.6 3.4 %fusion.98 = f32[4,64,512]{2,1,0:T(8,128)S(1)} fusion(bf16[512,4,64]{0,2,1:T(8,128)(2,1)S(1)} %bitcast.108, f32[4,512,512]{2,1,0:T(8,128)} %get-tuple-element.208, f32[4,512]{1,0:T(4,128)S(1)} %get-tuple-element.232, pred[512]{0:T(512)(128)(4,1)S(1)} %compare_reduce_fusion.2), kind=kOutput, calls=%fused_computation.7.clone.1 | convolution fusion | flops 139460608 | bytes 4989440 | tf_op jit(solution)/shard_map/while/body/eval_jaxpr/hqk,khd->qhd/dot_general | solution.py:71
  97.0 0.2 bitcast_add_fusion.2
  97.2 1.2 fusion.96
  98.4 1.1 constant_dynamic-slice_fusion.3
  99.5 0.1 copy.28
  99.7 2.9 %bitcast_reduce_fusion.2 = (f32[4,512]{1,0:T(4,128)S(1)}, f32[4,512,512]{2,1,0:T(8,128)}) fusion(pred[512]{0:T(512)(128)(4,1)S(1)} %compare_reduce_fusion.2, bf16[512,4,64]{0,2,1:T(8,128)(2,1)S(1)} %bitcast.105, bf16[512,4,64]{0,2,1:T(8,128)(2,1)S(1)} %get-tuple-element.237), kind=kOutput, calls=%fused_computation.1.clone.1 | convolution fusion | flops 137361408 | bytes 4727296 | tf_op jit(solution)/shard_map/while/body/eval_jaxpr/qhd,khd->hqk/dot_general | solution.py:63
  102.6 0.1 copy.29
  102.8 3.4 %fusion.98 = f32[4,64,512]{2,1,0:T(8,128)S(1)} fusion(bf16[512,4,64]{0,2,1:T(8,128)(2,1)S(1)} %bitcast.108, f32[4,512,512]{2,1,0:T(8,128)} %get-tuple-element.208, f32[4,512]{1,0:T(4,128)S(1)} %get-tuple-element.232, pred[512]{0:T(512)(128)(4,1)S(1)} %compare_reduce_fusion.2), kind=kOutput, calls=%fused_computation.7.clone.1 | convolution fusion | flops 139460608 | bytes 4989440 | tf_op jit(solution)/shard_map/while/body/eval_jaxpr/hqk,khd->qhd/dot_general | solution.py:71
  106.2 0.2 bitcast_add_fusion.2
  106.4 1.2 fusion.96
  107.6 0.1 fusion.31
  107.7 0.0 copy-start.3
  107.7 1.8 fusion.73
  109.5 0.0 all-gather.10.cloned.1.call-update
  109.6 0.0 reduce-scatter.2.cloned.1.call-start
  109.7 57.8 %all-gather.10.cloned.1.call-done = f32[2048,1024]{1,0:T(8,128)} async-done(((f32[512,1024]{1,0:T(8,128)}), f32[2048,1024]{1,0:T(8,128)}) %all-gather.10.cloned.1.call-update) | async-done | bytes 8388624 | tf_op jit(solution)/shard_map/all_gather | solution.py:112
  167.5 5.9 %reduce_sum.56 = f32[512,1024]{1,0:T(8,128)} reduce(f32[4,512,1024]{2,1,0:T(8,128)} %bitcast.106, f32[]{:T(128)} %constant.17.clone.1), dimensions={0}, to_apply=%region_6.7 | reduce | flops 1572864 | bytes 10485764 | tf_op jit(solution)/shard_map/reduce_sum | solution.py:113
  173.4 2.0 convert_reduce_fusion.1
  175.4 0.4 fusion.20
  175.9 0.5 fusion.27
  176.4 0.0 copy-start.8
  176.4 0.0 copy-start.11
  176.4 0.0 copy-start.12
  176.4 0.5 fusion.28
  177.0 3.4 %collective-permute-start = (bf16[15,256]{1,0:T(8,128)(2,1)S(1)}, bf16[15,256]{1,0:T(8,128)(2,1)S(1)}, u32[]{:S(2)}, u32[]{:S(2)}) collective-permute-start(bf16[15,256]{1,0:T(8,128)(2,1)S(1)} %get-tuple-element.117), channel_id=1, source_target_pairs={{0,4},{4,8},{8,12},{1,5},{5,9},{9,13},{2,6},{6,10},{10,14},{3,7},{... | collective-permute-start | bytes 23048 | tf_op jit(solution)/shard_map/ppermute | solution.py:16
  180.4 1.3 collective-permute-start.1
  181.7 0.0 collective-permute-done
  181.7 4.2 %collective-permute-done.1 = bf16[15,256]{1,0:T(8,128)(2,1)S(1)} collective-permute-done((bf16[15,256]{1,0:T(8,128)(2,1)S(1)}, bf16[15,256]{1,0:T(8,128)(2,1)S(1)}, u32[]{:S(2)}, u32[]{:S(2)}) %collective-permute-start.1) | collective-permute-done | bytes 7712 | tf_op jit(solution)/shard_map/ppermute | solution.py:19
  185.9 4.9 %convolution_convert_fusion = bf16[512,1024]{1,0:T(8,128)(2,1)} fusion(bf16[256,1024]{1,0:T(8,128)(2,1)S(1)} %copy-done.8, bf16[512,256]{1,0:T(8,128)(2,1)S(1)} %fusion.28, bf16[15,256]{1,0:T(8,128)(2,1)S(1)} %collective-permute-done.1, bf16[15,256]{1,0:T(8,128)(2,1)S(1)} %collective-permute-done, f32[256]{0:T(256)S(1)} %copy-done.11, ...), kind=kOutput, calls=%fused_computation.67 | convolution fusion | flops 293732352 | bytes 1884160 | tf_op jit(solution)/shard_map/dot_general | solution.py:130
  190.9 0.0 reduce-scatter.2.cloned.1.call-update
  190.9 24.1 %reduce-scatter.2.cloned.1.call-done = bf16[128,1024]{1,0:T(8,128)(2,1)} async-done(((bf16[512,1024]{1,0:T(8,128)(2,1)}), bf16[128,1024]{1,0:T(8,128)(2,1)}) %reduce-scatter.2.cloned.1.call-update) | async-done | bytes 262160 | tf_op jit(solution)/shard_map/reduce_scatter | solution.py:129
  215.0 1.7 add_convert_fusion
  (56 shorter events, 0.4 us)
Async XLA Ops:
  6.5 101.1 %copy-start = (bf16[256,1024]{1,0:T(8,128)(2,1)S(1)}, bf16[256,1024]{1,0:T(8,128)(2,1)}, u32[]{:S(2)}) copy-start(bf16[256,1024]{1,0:T(8,128)(2,1)} %param.21) | copy-start | bytes 1572868
  6.5 3.3 %copy-start.2 = (bf16[512,1024]{1,0:T(8,128)(2,1)S(1)}, bf16[512,1024]{1,0:T(8,128)(2,1)}, u32[]{:S(2)}) copy-start(bf16[512,1024]{1,0:T(8,128)(2,1)} %param.15) | copy-start | bytes 3145732
  6.5 3.3 %copy-start.9 = (f32[1024]{0:T(1024)S(1)}, f32[1024]{0:T(1024)}, u32[]{:S(2)}) copy-start(f32[1024]{0:T(1024)} %param.17) | copy-start | bytes 12292
  6.5 3.3 %copy-start.6 = (bf16[1024,256]{1,0:T(8,128)(2,1)S(1)}, bf16[1024,256]{1,0:T(8,128)(2,1)}, u32[]{:S(2)}) copy-start(bf16[1024,256]{1,0:T(8,128)(2,1)} %param.19) | copy-start | bytes 1572868
  6.5 35.4 %all-gather.6.cloned.1.call-start = ((), (), s32[]{:S(2)}) async-start(), calls=%async_computation.1 | async-start | bytes 1310720 | tf_op jit(solution)/shard_map/all_gather | solution.py:89
  9.8 1.4 copy-start.7
  11.1 1.4 copy-start.4
  11.1 59.8 %all-gather.8.cloned.1.call-start = ((), (), s32[]{:S(2)}) async-start(), calls=%async_computation.2 | async-start | bytes 1310720 | tf_op jit(solution)/shard_map/all_gather | solution.py:90
  12.4 155.1 %all-gather.10.cloned.1.call-start = ((), (), s32[]{:S(2)}) async-start(), calls=%async_computation.4 | async-start | bytes 10485760 | tf_op jit(solution)/shard_map/all_gather | solution.py:112
  75.2 3.6 %copy-start.1 = (f32[4,512,512]{2,1,0:T(8,128)S(1)}, f32[4,512,512]{2,1,0:T(8,128)}, u32[]{:S(2)}) copy-start(f32[4,512,512]{2,1,0:T(8,128)} %get-tuple-element.208) | copy-start | bytes 12582916 | tf_op jit(solution)/shard_map/while
  84.4 3.6 %copy-start.1 = (f32[4,512,512]{2,1,0:T(8,128)S(1)}, f32[4,512,512]{2,1,0:T(8,128)}, u32[]{:S(2)}) copy-start(f32[4,512,512]{2,1,0:T(8,128)} %get-tuple-element.208) | copy-start | bytes 12582916 | tf_op jit(solution)/shard_map/while
  93.6 3.6 %copy-start.1 = (f32[4,512,512]{2,1,0:T(8,128)S(1)}, f32[4,512,512]{2,1,0:T(8,128)}, u32[]{:S(2)}) copy-start(f32[4,512,512]{2,1,0:T(8,128)} %get-tuple-element.208) | copy-start | bytes 12582916 | tf_op jit(solution)/shard_map/while
  102.8 3.6 %copy-start.1 = (f32[4,512,512]{2,1,0:T(8,128)S(1)}, f32[4,512,512]{2,1,0:T(8,128)}, u32[]{:S(2)}) copy-start(f32[4,512,512]{2,1,0:T(8,128)} %get-tuple-element.208) | copy-start | bytes 12582916 | tf_op jit(solution)/shard_map/while
  107.7 1.9 copy-start.3
  109.6 105.5 %reduce-scatter.2.cloned.1.call-start = ((), (), s32[]{:S(2)}) async-start(), calls=%async_computation.3 | async-start | bytes 1310720 | tf_op jit(solution)/shard_map/reduce_scatter | solution.py:129
  173.4 2.4 %copy-start.5 = (bf16[2,1024,256]{2,1,0:T(8,128)(2,1)S(1)}, bf16[2,1024,256]{2,1,0:T(8,128)(2,1)}, u32[]{:S(2)}) copy-start(bf16[2,1024,256]{2,1,0:T(8,128)(2,1)} %param.23) | copy-start | bytes 3145732
  173.4 2.4 %copy-start.10 = (f32[1024]{0:T(1024)S(1)}, f32[1024]{0:T(1024)}, u32[]{:S(2)}) copy-start(f32[1024]{0:T(1024)} %param.22) | copy-start | bytes 12292
  176.4 9.5 %copy-start.8 = (bf16[256,1024]{1,0:T(8,128)(2,1)S(1)}, bf16[256,1024]{1,0:T(8,128)(2,1)}, u32[]{:S(2)}) copy-start(bf16[256,1024]{1,0:T(8,128)(2,1)} %param.27) | copy-start | bytes 1572868
  176.4 9.5 %copy-start.11 = (f32[256]{0:T(256)S(1)}, f32[256]{0:T(256)}, u32[]{:S(2)}) copy-start(f32[256]{0:T(256)} %param.26) | copy-start | bytes 3076
  176.4 9.5 %copy-start.12 = (f32[256]{0:T(256)S(1)}, f32[256]{0:T(256)}, u32[]{:S(2)}) copy-start(f32[256]{0:T(256)} %param.25) | copy-start | bytes 3076
  177.0 4.7 %collective-permute-start = (bf16[15,256]{1,0:T(8,128)(2,1)S(1)}, bf16[15,256]{1,0:T(8,128)(2,1)S(1)}, u32[]{:S(2)}, u32[]{:S(2)}) collective-permute-start(bf16[15,256]{1,0:T(8,128)(2,1)S(1)} %get-tuple-element.117), channel_id=1, source_target_pairs={{0,4},{4,8},{8,12},{1,5},{5,9},{9,13},{2,6},{6,10},{10,14},{3,7},{... | collective-permute-start | bytes 23048 | tf_op jit(solution)/shard_map/ppermute | solution.py:16
  180.4 5.5 %collective-permute-start.1 = (bf16[15,256]{1,0:T(8,128)(2,1)S(1)}, bf16[15,256]{1,0:T(8,128)(2,1)S(1)}, u32[]{:S(2)}, u32[]{:S(2)}) collective-permute-start(bf16[15,256]{1,0:T(8,128)(2,1)S(1)} %get-tuple-element.118), channel_id=1, source_target_pairs={{4,0},{8,4},{12,8},{5,1},{9,5},{13,9},{6,2},{10,6},{14,10},{7,3},{... | collective-permute-start | bytes 23048 | tf_op jit(solution)/shard_map/ppermute | solution.py:19
Sparse Core Ops, SparseCore 0:
  11.2 30.6 all-gather.5
  43.5 27.3 all-gather.7
  109.7 57.7 all-gather.9
  191.0 23.9 reduce-scatter.1
